TPU v7x, 32 devices: a whole 2x2x4 slice. The times are simulated.
32 devices in a mesh: dp: 4 (over y, x), seq: 8 (over z, core).
Axes of the slice: x: 2, y: 2, z: 4, core: 2. Of those that a mesh axis runs over, the one named last changes fastest.
Arguments:
- queries: bfloat16 [4096, 4096], P(('dp', 'seq')), may hold values from -30 to 30
- keys: bfloat16 [4096, 512], P(('dp', 'seq')), may hold values from -7.5 to 7.5
- values: bfloat16 [4096, 512], P(('dp', 'seq')), may hold values from -4 to 4
- doc_lengths: int32 [4, 32], replicated, may hold values from 0 to 128, as said below
- loader_order: int32 [4, 4], replicated, may hold values from 0 to 3, each once within a row
- grad_out: bfloat16 [4096, 4096], P(('dp', 'seq')), may hold values from -4 to 4
Outputs:
- attended: bfloat16 [4096, 4096], P(('dp', 'seq'))
- grad_queries: bfloat16 [4096, 4096], P(('dp', 'seq'))
- grad_keys: bfloat16 [4096, 512], P(('dp', 'seq'))
- grad_values: bfloat16 [4096, 512], P(('dp', 'seq'))
Inputs may be any that keep to these rules, and one draw needn't show every extreme that they name: `doc_lengths`: the documents of a bin fill its first positions in order; each is 32 to 128 long except that a bin's last may be shorter, and the entries after it are 0. The first document of every bin is 128 long; every bin holds 512 tokens or more, and some bin exactly 1024.
All inputs are finite; a program needn't handle non-finite values.
Results may differ from a plain program's by a relative error of at most 0.0067.
Values may be sent and summed in bfloat16 or wider, within the bound.
A program may use at most 64 MiB of HBM per device.

v0:
```python
import jax
import jax.numpy as jnp
from jax import lax
from jax.sharding import PartitionSpec as P

QH = 32
KVH = 4
HD = 128


def bin_layout(lengths, row_count):
    doc_ends = jnp.cumsum(lengths, axis=-1)
    filled_to = doc_ends[..., -1]
    positions = jnp.arange(row_count, dtype=jnp.int32)
    doc_of = jnp.sum((doc_ends[..., None, :] <= positions[:, None]).astype(jnp.int32), axis=-1)
    marked = jnp.where(positions < filled_to[..., None], doc_of, -1 - positions)
    return (filled_to, marked)


def loader_runs(filled_to, order_row, source, capacity):
    bin_index = jnp.arange(filled_to.shape[0], dtype=jnp.int32)
    counts = jnp.clip(filled_to - source * capacity, 0, capacity)
    choose_run = (order_row[:, None] == bin_index[None, :]).astype(jnp.int32)
    ordered = jnp.sum(choose_run * counts[None, :], axis=1)
    run_start = jnp.cumsum(ordered) - ordered
    return (ordered, run_start)


def loader_targets(ordered, run_start, order_row, capacity, row_count):
    positions = jnp.arange(row_count, dtype=jnp.int32)
    inside = (positions[:, None] >= run_start[None, :]) & (
        positions[:, None] < (run_start + ordered)[None, :]
    )
    target = order_row * capacity - run_start
    slot_index = jnp.sum(jnp.where(inside, target[None, :], 0), axis=1) + positions
    return (slot_index, jnp.any(inside, axis=1))


def local(queries, keys, values, doc_lengths, loader_order, grad_out):
    dp_count = lax.axis_size("dp")
    seq_count = lax.axis_size("seq")
    tokens_here = queries.shape[0]
    loader_rows = tokens_here * seq_count
    capacity = loader_rows // dp_count
    block_rows = loader_rows // 8
    heads_here = QH // seq_count
    group_devices = seq_count // KVH
    loader_id = lax.axis_index("dp")
    score_scale = HD ** (-0.5)
    wide_keys = jnp.broadcast_to(
        keys.reshape(tokens_here, KVH, 1, HD), (tokens_here, KVH, group_devices, HD)
    ).reshape(tokens_here, seq_count * HD)
    wide_values = jnp.broadcast_to(
        values.reshape(tokens_here, KVH, 1, HD), (tokens_here, KVH, group_devices, HD)
    ).reshape(tokens_here, seq_count * HD)
    head_query, head_keys, head_values, incoming = (
        lax.all_to_all(queries, "seq", split_axis=1, concat_axis=0, tiled=True),
        lax.all_to_all(wide_keys, "seq", split_axis=1, concat_axis=0, tiled=True),
        lax.all_to_all(wide_values, "seq", split_axis=1, concat_axis=0, tiled=True),
        lax.all_to_all(grad_out, "seq", split_axis=1, concat_axis=0, tiled=True),
    )
    all_filled = jnp.sum(doc_lengths, axis=1)
    order_row = lax.dynamic_index_in_dim(loader_order, loader_id, 0, keepdims=False)
    ordered, run_start = loader_runs(all_filled, order_row, loader_id, capacity)
    slot_index, placed = loader_targets(ordered, run_start, order_row, capacity, loader_rows)
    slot_index = jnp.where(placed, slot_index, dp_count * capacity)
    payload = jnp.concatenate([head_query, head_keys, head_values], axis=1)
    outgoing = (
        jnp.zeros((dp_count * capacity, payload.shape[1]), payload.dtype)
        .at[slot_index]
        .set(payload, mode="drop")
    )
    arrived = lax.all_to_all(outgoing, "dp", split_axis=0, concat_axis=0, tiled=True)
    query_width = heads_here * HD
    bin_query = arrived[:, :query_width].reshape(loader_rows, heads_here, HD)
    front_zeros = jnp.zeros((block_rows, HD), jnp.bfloat16)
    keys_pad = jnp.concatenate([front_zeros, arrived[:, query_width : query_width + HD]], axis=0)
    values_pad = jnp.concatenate([front_zeros, arrived[:, query_width + HD :]], axis=0)
    grad_bin = incoming.reshape(loader_rows, heads_here, HD)
    own_lengths = lax.dynamic_index_in_dim(doc_lengths, loader_id, 0, keepdims=False)
    own_filled, marked = bin_layout(own_lengths, loader_rows)
    marked_pad = jnp.concatenate(
        [-2 * loader_rows - jnp.arange(block_rows, dtype=jnp.int32), marked]
    )
    query_rows = jnp.arange(block_rows, dtype=jnp.int32)[:, None] + block_rows
    window_cols = jnp.arange(2 * block_rows, dtype=jnp.int32)[None, :]

    def tile(running, tile_number):
        tile_start = tile_number * block_rows
        query_tile = lax.dynamic_slice_in_dim(bin_query, tile_start, block_rows, 0)
        grad_rows = lax.dynamic_slice_in_dim(grad_bin, tile_start, block_rows, 0)
        marked_query = lax.dynamic_slice_in_dim(marked, tile_start, block_rows, 0)
        keys_window = lax.dynamic_slice_in_dim(keys_pad, tile_start, 2 * block_rows, 0)
        values_window = lax.dynamic_slice_in_dim(values_pad, tile_start, 2 * block_rows, 0)
        marked_window = lax.dynamic_slice_in_dim(marked_pad, tile_start, 2 * block_rows, 0)
        allowed = (marked_query[:, None] == marked_window[None, :]) & (window_cols <= query_rows)
        scores = (
            jnp.einsum("qhd,kd->hqk", query_tile, keys_window, preferred_element_type=jnp.float32)
            * score_scale
        )
        scores = jnp.where(allowed[None], scores, -jnp.inf)
        row_peak = jnp.max(scores, axis=-1, keepdims=True)
        row_total = jnp.sum(jnp.exp(scores - row_peak), axis=-1, keepdims=True)
        probs_full = jnp.exp(scores - (row_peak + jnp.log(row_total)))
        probs_half = probs_full.astype(jnp.bfloat16)
        filled_slot = marked_query >= 0
        attended32 = jnp.einsum(
            "hqk,kd->qhd", probs_half, values_window, preferred_element_type=jnp.float32
        )
        attended32 = jnp.where(filled_slot[:, None, None], attended32, jnp.float32(0.0))
        grad_here = jnp.where(filled_slot[:, None, None], grad_rows, jnp.zeros((), jnp.bfloat16))
        grad_probs = jnp.einsum(
            "qhd,kd->hqk", grad_here, values_window, preferred_element_type=jnp.float32
        )
        row_dot = jnp.transpose(
            jnp.sum(grad_here.astype(jnp.float32) * attended32, axis=-1), (1, 0)
        )[..., None]
        grad_half = (probs_full * (grad_probs - row_dot)).astype(jnp.bfloat16)
        grad_query = (
            jnp.einsum("hqk,kd->qhd", grad_half, keys_window, preferred_element_type=jnp.float32)
            * score_scale
        )
        key_terms = (
            jnp.einsum("hqk,qhd->kd", grad_half, query_tile, preferred_element_type=jnp.float32)
            * score_scale
        )
        value_terms = jnp.einsum(
            "hqk,qhd->kd", probs_half, grad_here, preferred_element_type=jnp.float32
        )
        both_terms = jnp.concatenate([key_terms, value_terms], axis=1)
        running = lax.dynamic_update_slice_in_dim(
            running,
            lax.dynamic_slice_in_dim(running, tile_start, 2 * block_rows, 0) + both_terms,
            tile_start,
            0,
        )
        return (
            running,
            (
                attended32.astype(jnp.bfloat16).reshape(block_rows, query_width),
                grad_query.astype(jnp.bfloat16).reshape(block_rows, query_width),
            ),
        )

    empty_total = jnp.zeros((block_rows + loader_rows, 2 * HD), jnp.float32)
    kv_total, tiles_out = lax.scan(tile, empty_total, jnp.arange(8, dtype=jnp.int32))
    attended_half = tiles_out[0].reshape(loader_rows, query_width)
    grad_query_half = tiles_out[1].reshape(loader_rows, query_width)
    attended, grad_queries = (
        lax.all_to_all(attended_half, "seq", split_axis=0, concat_axis=1, tiled=True),
        lax.all_to_all(grad_query_half, "seq", split_axis=0, concat_axis=1, tiled=True),
    )
    kv_local = kv_total[block_rows:]
    kv_back = lax.all_to_all(kv_local, "seq", split_axis=0, concat_axis=0, tiled=True)
    summed = jnp.sum(kv_back.reshape(KVH, group_devices, tokens_here, 2 * HD), axis=1)
    grad_keys = (
        jnp.transpose(summed[:, :, :HD], (1, 0, 2))
        .reshape(tokens_here, KVH * HD)
        .astype(jnp.bfloat16)
    )
    grad_values = (
        jnp.transpose(summed[:, :, HD:], (1, 0, 2))
        .reshape(tokens_here, KVH * HD)
        .astype(jnp.bfloat16)
    )
    return (attended, grad_queries, grad_keys, grad_values)


def solution(mesh):
    placed = (
        P(("dp", "seq"), None),
        P(("dp", "seq"), None),
        P(("dp", "seq"), None),
        P(),
        P(),
        P(("dp", "seq"), None),
    )
    return jax.shard_map(
        local,
        mesh=mesh,
        in_specs=placed,
        out_specs=(
            P(("dp", "seq"), None),
            P(("dp", "seq"), None),
            P(("dp", "seq"), None),
            P(("dp", "seq"), None),
        ),
        check_vma=False,
    )
```

profile of v0, /device:TPU:0, one launch (start us, length us, event | category | flops | bytes accessed | tf_op | source)
XLA Modules:
  0.0 282.5 jit_solution(15179628783018283675)
XLA Ops:
  2.3 6.3 %all-to-all-start.1 = ((bf16[128,8,128]{2,0,1:T(8,128)(2,1)}), bf16[128,8,128]{2,0,1:T(8,128)(2,1)S(1)}, u32[]{:S(2)}, u32[]{:S(2)}) async-start(bf16[128,8,128]{2,0,1:T(8,128)(2,1)} %bitcast.13), calls=%async_computation.1 | async-start | bytes 524288 | tf_op jit(solution)/shard_map/all_to_all | solution.py:58
  9.6 8.8 %all-to-all-done.1 = bf16[128,8,128]{2,0,1:T(8,128)(2,1)S(1)} async-done(((bf16[128,8,128]{2,0,1:T(8,128)(2,1)}), bf16[128,8,128]{2,0,1:T(8,128)(2,1)S(1)}, u32[]{:S(2)}, u32[]{:S(2)}) %all-to-all-start.1) | async-done | bytes 262176 | tf_op jit(solution)/shard_map/all_to_all | solution.py:58
  19.1 3.4 %all-to-all-start.2 = ((bf16[128,8,128]{2,0,1:T(8,128)(2,1)}), bf16[128,8,128]{2,0,1:T(8,128)(2,1)S(1)}, u32[]{:S(2)}, u32[]{:S(2)}) async-start(bf16[128,8,128]{2,0,1:T(8,128)(2,1)} %bitcast.16), calls=%async_computation.2 | async-start | bytes 524288 | tf_op jit(solution)/shard_map/all_to_all | solution.py:59
  22.5 1.3 copy.119
  23.9 8.3 %all-to-all-done.2 = bf16[128,8,128]{2,0,1:T(8,128)(2,1)S(1)} async-done(((bf16[128,8,128]{2,0,1:T(8,128)(2,1)}), bf16[128,8,128]{2,0,1:T(8,128)(2,1)S(1)}, u32[]{:S(2)}, u32[]{:S(2)}) %all-to-all-start.2) | async-done | bytes 262176 | tf_op jit(solution)/shard_map/all_to_all | solution.py:59
  32.2 3.6 %all-to-all-start = ((bf16[128,8,512]{0,2,1:T(8,128)(2,1)}), bf16[128,8,512]{0,2,1:T(8,128)(2,1)S(1)}, u32[]{:S(2)}, u32[]{:S(2)}) async-start(bf16[128,8,512]{0,2,1:T(8,128)(2,1)} %bitcast.10), calls=%async_computation | async-start | bytes 2097152 | tf_op jit(solution)/shard_map/all_to_all | solution.py:57
  35.8 1.3 copy.124
  37.1 25.2 %all-to-all-done = bf16[128,8,512]{0,2,1:T(8,128)(2,1)S(1)} async-done(((bf16[128,8,512]{0,2,1:T(8,128)(2,1)}), bf16[128,8,512]{0,2,1:T(8,128)(2,1)S(1)}, u32[]{:S(2)}, u32[]{:S(2)}) %all-to-all-start) | async-done | bytes 1048608 | tf_op jit(solution)/shard_map/all_to_all | solution.py:57
  62.3 3.6 %all-to-all-start.4 = ((bf16[128,8,512]{0,2,1:T(8,128)(2,1)}), bf16[128,8,512]{0,2,1:T(8,128)(2,1)S(1)}, u32[]{:S(2)}, u32[]{:S(2)}) async-start(bf16[128,8,512]{0,2,1:T(8,128)(2,1)} %bitcast.22), calls=%async_computation.4 | async-start | bytes 2097152 | tf_op jit(solution)/shard_map/all_to_all | solution.py:60
  67.2 6.9 %scatter_custom_fusion = bf16[1024,768]{1,0:T(8,128)(2,1)} fusion(s32[1024]{0:T(1024)S(1)} %bitcast.161, bf16[1024,128]{1,0:T(8,128)(2,1)} %bitcast.154, bf16[]{:T(256)} %constant.78, bf16[1024,128]{1,0:T(8,128)(2,1)S(1)} %bitcast.153, bf16[1024,512]{1,0:T(8,128)(2,1)S(1)} %bitcast.151, bf16[]{:T(256)} %constant.33.clone.1), kind=kCustom, calls=%fused_computation.52 | custom fusion | flops 4718592 | bytes 3145732 | tf_op jit(solution)/shard_map/scatter | solution.py:71
  74.0 18.3 %all-to-all-done.4 = bf16[128,8,512]{0,2,1:T(8,128)(2,1)S(1)} async-done(((bf16[128,8,512]{0,2,1:T(8,128)(2,1)}), bf16[128,8,512]{0,2,1:T(8,128)(2,1)S(1)}, u32[]{:S(2)}, u32[]{:S(2)}) %all-to-all-start.4) | async-done | bytes 1048608 | tf_op jit(solution)/shard_map/all_to_all | solution.py:60
  92.4 3.7 %all-to-all-start.3 = ((bf16[4,256,768]{2,1,0:T(8,128)(2,1)}), bf16[4,256,768]{2,1,0:T(8,128)(2,1)S(1)}, u32[]{:S(2)}, u32[]{:S(2)}) async-start(bf16[4,256,768]{2,1,0:T(8,128)(2,1)} %bitcast.19), calls=%async_computation.3 | async-start | bytes 3145728 | tf_op jit(solution)/shard_map/all_to_all | solution.py:73
  97.6 1.6 copy.125
  99.3 1.5 reshape.208
  100.8 14.4 %all-to-all-done.3 = bf16[4,256,768]{2,1,0:T(8,128)(2,1)S(1)} async-done(((bf16[4,256,768]{2,1,0:T(8,128)(2,1)}), bf16[4,256,768]{2,1,0:T(8,128)(2,1)S(1)}, u32[]{:S(2)}, u32[]{:S(2)}) %all-to-all-start.3) | async-done | bytes 1572896 | tf_op jit(solution)/shard_map/all_to_all | solution.py:73
  116.4 2.3 copy.159
  120.6 68.7 %while.15 = (s32[]{:T(128)}, f32[1152,256]{1,0:T(8,128)S(1)}, bf16[8,128,512]{1,2,0:T(8,128)(2,1)}, bf16[8,128,512]{1,2,0:T(8,128)(2,1)}, s32[8]{0:T(128)S(1)}, ...) while((s32[]{:T(128)}, f32[1152,256]{1,0:T(8,128)S(1)}, ...), condition=%wide.region_12.13_spmd.clone, body=%wide.region_8.12_spmd.clone.sunk | while | flops 203947264 | bytes 8353704 | solution.py:146
  189.3 30.1 %all_to_all.126 = bf16[8,128,512]{1,2,0:T(8,128)(2,1)S(1)} all-to-all(bf16[8,128,512]{1,2,0:T(8,128)(2,1)} %get-tuple-element.74), channel_id=1, replica_groups=mesh['dp'=4,'seq'=8] {'seq'}, dimensions={0} | all-to-all | bytes 2097152 | tf_op jit(solution)/shard_map/all_to_all | solution.py:151
  219.4 3.6 %all-to-all-start.5 = ((bf16[8,128,512]{1,2,0:T(8,128)(2,1)}), bf16[8,128,512]{1,2,0:T(8,128)(2,1)S(1)}, u32[]{:S(2)}, u32[]{:S(2)}) async-start(bf16[8,128,512]{1,2,0:T(8,128)(2,1)} %get-tuple-element.73), calls=%async_computation.5 | async-start | bytes 2097152 | tf_op jit(solution)/shard_map/all_to_all | solution.py:150
  224.0 2.5 copy.132
  226.5 22.9 %all-to-all-done.5 = bf16[8,128,512]{1,2,0:T(8,128)(2,1)S(1)} async-done(((bf16[8,128,512]{1,2,0:T(8,128)(2,1)}), bf16[8,128,512]{1,2,0:T(8,128)(2,1)S(1)}, u32[]{:S(2)}, u32[]{:S(2)}) %all-to-all-start.5) | async-done | bytes 1048608 | tf_op jit(solution)/shard_map/all_to_all | solution.py:150
  250.4 3.6 %all-to-all-start.7 = ((f32[8,128,256]{1,2,0:T(8,128)}), f32[8,128,256]{1,2,0:T(8,128)S(1)}, u32[]{:S(2)}, u32[]{:S(2)}) async-start(f32[8,128,256]{1,2,0:T(8,128)} %copy.132), calls=%async_computation.7 | async-start | bytes 2097152 | tf_op jit(solution)/shard_map/all_to_all | solution.py:154
  254.0 1.3 copy.148
  256.6 23.9 %all-to-all-done.7 = f32[8,128,256]{1,2,0:T(8,128)S(1)} async-done(((f32[8,128,256]{1,2,0:T(8,128)}), f32[8,128,256]{1,2,0:T(8,128)S(1)}, u32[]{:S(2)}, u32[]{:S(2)}) %all-to-all-start.7) | async-done | bytes 1048608 | tf_op jit(solution)/shard_map/all_to_all | solution.py:154
  (211 shorter events, 77.1 us)
Async XLA Ops:
  0.6 0.9 copy-start
  0.6 21.9 %copy-start.4 = (bf16[128,4096]{1,0:T(8,128)(2,1)S(1)}, bf16[128,4096]{1,0:T(8,128)(2,1)}, u32[]{:S(2)}) copy-start(bf16[128,4096]{1,0:T(8,128)(2,1)} %param.8) | copy-start | bytes 3145732
  2.3 16.1 %all-to-all-start.1 = ((bf16[128,8,128]{2,0,1:T(8,128)(2,1)}), bf16[128,8,128]{2,0,1:T(8,128)(2,1)S(1)}, u32[]{:S(2)}, u32[]{:S(2)}) async-start(bf16[128,8,128]{2,0,1:T(8,128)(2,1)} %bitcast.13), calls=%async_computation.1 | async-start | bytes 524288 | tf_op jit(solution)/shard_map/all_to_all | solution.py:58
  19.1 13.1 %all-to-all-start.2 = ((bf16[128,8,128]{2,0,1:T(8,128)(2,1)}), bf16[128,8,128]{2,0,1:T(8,128)(2,1)S(1)}, u32[]{:S(2)}, u32[]{:S(2)}) async-start(bf16[128,8,128]{2,0,1:T(8,128)(2,1)} %bitcast.16), calls=%async_computation.2 | async-start | bytes 524288 | tf_op jit(solution)/shard_map/all_to_all | solution.py:59
  23.9 11.9 %copy-start.5 = (bf16[128,4096]{1,0:T(8,128)(2,1)S(1)}, bf16[128,4096]{1,0:T(8,128)(2,1)}, u32[]{:S(2)}) copy-start(bf16[128,4096]{1,0:T(8,128)(2,1)} %param.13) | copy-start | bytes 3145732
  32.2 4.9 %copy-start.3 = (bf16[128,8,128]{2,0,1:T(8,128)(2,1)}, bf16[128,8,128]{2,0,1:T(8,128)(2,1)S(1)}, u32[]{:S(2)}) copy-start(bf16[128,8,128]{2,0,1:T(8,128)(2,1)S(1)} %all-to-all-done.2) | copy-start | bytes 786436
  32.2 30.1 %all-to-all-start = ((bf16[128,8,512]{0,2,1:T(8,128)(2,1)}), bf16[128,8,512]{0,2,1:T(8,128)(2,1)S(1)}, u32[]{:S(2)}, u32[]{:S(2)}) async-start(bf16[128,8,512]{0,2,1:T(8,128)(2,1)} %bitcast.10), calls=%async_computation | async-start | bytes 2097152 | tf_op jit(solution)/shard_map/all_to_all | solution.py:57
  37.1 28.8 %copy-start.6 = (s32[4,32]{1,0:T(4,128)S(1)}, s32[4,32]{1,0:T(4,128)}, u32[]{:S(2)}) copy-start(s32[4,32]{1,0:T(4,128)} %param.11) | copy-start | bytes 1540
  37.1 28.9 %copy-start.7 = (s32[4,4]{1,0:T(4,128)S(1)}, s32[4,4]{1,0:T(4,128)}, u32[]{:S(2)}) copy-start(s32[4,4]{1,0:T(4,128)} %param.12) | copy-start | bytes 196
  62.3 30.1 %all-to-all-start.4 = ((bf16[128,8,512]{0,2,1:T(8,128)(2,1)}), bf16[128,8,512]{0,2,1:T(8,128)(2,1)S(1)}, u32[]{:S(2)}, u32[]{:S(2)}) async-start(bf16[128,8,512]{0,2,1:T(8,128)(2,1)} %bitcast.22), calls=%async_computation.4 | async-start | bytes 2097152 | tf_op jit(solution)/shard_map/all_to_all | solution.py:60
  92.4 22.9 %all-to-all-start.3 = ((bf16[4,256,768]{2,1,0:T(8,128)(2,1)}), bf16[4,256,768]{2,1,0:T(8,128)(2,1)S(1)}, u32[]{:S(2)}, u32[]{:S(2)}) async-start(bf16[4,256,768]{2,1,0:T(8,128)(2,1)} %bitcast.19), calls=%async_computation.3 | async-start | bytes 3145728 | tf_op jit(solution)/shard_map/all_to_all | solution.py:73
  219.4 30.1 %all-to-all-start.5 = ((bf16[8,128,512]{1,2,0:T(8,128)(2,1)}), bf16[8,128,512]{1,2,0:T(8,128)(2,1)S(1)}, u32[]{:S(2)}, u32[]{:S(2)}) async-start(bf16[8,128,512]{1,2,0:T(8,128)(2,1)} %get-tuple-element.73), calls=%async_computation.5 | async-start | bytes 2097152 | tf_op jit(solution)/shard_map/all_to_all | solution.py:150
  249.4 1.0 copy-start.1
  250.4 30.1 %all-to-all-start.7 = ((f32[8,128,256]{1,2,0:T(8,128)}), f32[8,128,256]{1,2,0:T(8,128)S(1)}, u32[]{:S(2)}, u32[]{:S(2)}) async-start(f32[8,128,256]{1,2,0:T(8,128)} %copy.132), calls=%async_computation.7 | async-start | bytes 2097152 | tf_op jit(solution)/shard_map/all_to_all | solution.py:154
  254.0 1.3 copy-start.2
where the time goes:
time: 285 us; the launch traced here: 282 us
  waiting for transfers between devices  122 us (43%)
  matrix products  46.5 us (16%)
  local copies, waits for them, and re-layouts  38.2 us (13%)
  blocking collectives  30.1 us (11%)
  starting transfers between devices  27.7 us (10%)
  other arithmetic  11.1 us (4%)
  loops' own time  6.08 us (2%)
    all_to_all x1, blocking collectives, local(): lax.all_to_all(grad_query_half, 'seq', split_axis=0, concat_axis=1, tiled...  30.1 us
    all_to_all x1, waiting for transfers between devices, local(): lax.all_to_all(queries, 'seq', split_axis=1, concat_axis=0, tiled=True)  25.2 us
    all_to_all x1, waiting for transfers between devices, local(): lax.all_to_all(kv_local, 'seq', split_axis=0, concat_axis=0, tiled=True)  23.9 us
    all_to_all x1, waiting for transfers between devices, local(): lax.all_to_all(attended_half, 'seq', split_axis=0, concat_axis=1, tiled=T...  22.9 us
    all_to_all x1, waiting for transfers between devices, local(): lax.all_to_all(grad_out, 'seq', split_axis=1, concat_axis=0, tiled=True)  18.3 us
    all_to_all x1, waiting for transfers between devices, local(): lax.all_to_all(outgoing, 'dp', split_axis=0, concat_axis=0, tiled=True)  14.4 us
    dot_general x8, matrix products, tile(): jnp.einsum('qhd,kd->hqk', query_tile, keys_window, preferred_element_type...  9.7 us
    dot_general x8, matrix products, tile(): jnp.einsum('hqk,qhd->kd', grad_half, query_tile, preferred_element_type=j...  9.08 us
  transfers between devices with their start and end apart: 7, of which 7 were waited for; matrix products, arithmetic and copies ran while one was open for 8% of the time, Pallas kernels for 0%

commit v1 on v0

v1 whole, which is shorter than its diff:
```python
import functools

import jax
import jax.numpy as jnp
from jax import lax
from jax.experimental import pallas as pl
from jax.experimental.pallas import tpu as pltpu
from jax.sharding import PartitionSpec as P

QH = 32
KVH = 4
HD = 128
BLOCKS = 8
MESH = pl.DeviceIdType.MESH
F32 = jnp.float32
BF16 = jnp.bfloat16


def dot_nt(a, b):
    return lax.dot_general(a, b, (((1,), (1,)), ((), ())), preferred_element_type=F32)


def dot_nn(a, b):
    return lax.dot_general(a, b, (((1,), (0,)), ((), ())), preferred_element_type=F32)


def dot_tn(a, b):
    return lax.dot_general(a, b, (((0,), (0,)), ((), ())), preferred_element_type=F32)


def kernel(
    dp_n,
    seq_n,
    q_ref,
    k_ref,
    v_ref,
    len_ref,
    order_ref,
    g_ref,
    att_ref,
    gq_ref,
    gk_ref,
    gv_ref,
    kv_all,
    rows_in,
    stage,
    slots,
    halo,
    own_terms,
    back_out,
    back_in,
    start_s,
    count_s,
    s1_send,
    s1_recv,
    s2_send,
    s2_recv,
    halo_send,
    halo_recv,
    back_send,
    back_recv,
):
    tokens = q_ref.shape[0]
    loader_rows = tokens * seq_n
    capacity = loader_rows // dp_n
    per = capacity // tokens
    n = dp_n * per
    reach = loader_rows // BLOCKS // tokens
    qw = QH * HD // n
    heads = qw // HD
    kv_blocks = 2 * KVH
    repeat = n // kv_blocks
    docs = len_ref.shape[1]
    scale = HD ** (-0.5)
    d0 = lax.axis_index("dp")
    i0 = lax.axis_index("seq")
    source = i0 // per
    f_me = d0 * per + lax.rem(i0, per)

    def greet(t, carry):
        dd, ii = t // seq_n, lax.rem(t, seq_n)

        @pl.when(jnp.logical_or(dd != d0, ii != i0))
        def _():
            pl.semaphore_signal(
                pltpu.get_barrier_semaphore(), 1, device_id={"dp": dd, "seq": ii}, device_id_type=MESH
            )

        return carry

    lax.fori_loop(0, dp_n * seq_n, greet, 0)
    kv_all[:, : KVH * HD] = k_ref[...]
    kv_all[:, KVH * HD :] = v_ref[...]
    pl.semaphore_wait(pltpu.get_barrier_semaphore(), dp_n * seq_n - 1)

    def remote(src, dst, send, recv, dd, ii):
        return pltpu.make_async_remote_copy(
            src_ref=src,
            dst_ref=dst,
            send_sem=send,
            recv_sem=recv,
            device_id={"dp": dd, "seq": ii},
            device_id_type=MESH,
        )

    def start_copy(src, dst, send, recv, dd, ii):
        here = jnp.logical_and(dd == d0, ii == i0)

        @pl.when(here)
        def _():
            pltpu.make_async_copy(src, dst, recv).start()

        @pl.when(jnp.logical_not(here))
        def _():
            remote(src, dst, send, recv, dd, ii).start()

    def wait_sent(src, dst, send, recv, dd, ii):
        @pl.when(jnp.logical_or(dd != d0, ii != i0))
        def _():
            remote(src, dst, send, recv, dd, ii).wait_send()

    def wait_here(dst, recv):
        pltpu.make_async_copy(dst, dst, recv).wait()

    first = []
    my_rows = pl.ds(pl.multiple_of(i0 * tokens, tokens), tokens)
    for t in range(n):
        f = lax.rem(i0 + t, n)
        dd, ii = f // per, d0 * per + lax.rem(f, per)
        src_kv = kv_all.at[:, pl.ds(pl.multiple_of((f // repeat) * HD, HD), HD)]
        src_q = q_ref.at[:, pl.ds(pl.multiple_of(f * qw, HD), qw)]
        dst_kv = rows_in.at[my_rows, pl.ds(qw, HD)]
        dst_q = rows_in.at[my_rows, pl.ds(0, qw)]
        first.append((src_kv, dst_kv, s1_send.at[1, t], s1_recv.at[1, i0], dd, ii))
        first.append((src_q, dst_q, s1_send.at[0, t], s1_recv.at[0, i0], dd, ii))
        start_copy(*first[-2])
        start_copy(*first[-1])

    filled = []
    for b in range(dp_n):
        total = len_ref[b, 0]
        for d in range(1, docs):
            total = total + len_ref[b, d]
        filled.append(total)
    counts = [jnp.clip(x - source * capacity, 0, capacity) for x in filled]
    order = [order_ref[source, k] for k in range(dp_n)]
    place = []
    for b in range(dp_n):
        at = jnp.int32(0)
        for k in range(dp_n):
            at = at + jnp.where(order[k] == b, k, 0)
        place.append(at)
    for b in range(dp_n):
        at = jnp.int32(0)
        for c in range(dp_n):
            at = at + jnp.where(place[c] < place[b], counts[c], 0)
        start_s[b] = at
        count_s[b] = counts[b]

    row = lax.broadcasted_iota(jnp.int32, (tokens, 1), 0) + i0 * tokens
    low = jnp.zeros((tokens, 1), jnp.int32)
    end = jnp.int32(0)
    for d in range(docs):
        end = end + len_ref[d0, d]
        low = jnp.where(row >= end, end, low)
    is_filled = row < end
    low = jnp.where(is_filled, low, row)
    window = (reach + 1) * tokens
    col = lax.broadcasted_iota(jnp.int32, (tokens, window), 1) + (i0 - reach) * tokens
    allowed = jnp.logical_and(col >= low, col <= row)
    bias = jnp.where(allowed, 0.0, -jnp.inf).astype(F32)

    for d in range(1, reach + 1):

        @pl.when(i0 < d)
        def _():
            halo[d - 1] = jnp.zeros(halo.shape[1:], BF16)

    for j in range(seq_n):
        there = pl.ds(j * tokens, tokens)
        wait_here(rows_in.at[there, pl.ds(qw, HD)], s1_recv.at[1, j])
        wait_here(rows_in.at[there, pl.ds(0, qw)], s1_recv.at[0, j])

    second = []
    u = lax.broadcasted_iota(jnp.int32, (tokens, loader_rows), 0)
    r = lax.broadcasted_iota(jnp.int32, (tokens, loader_rows), 1)
    diff = r - u
    u_col = lax.broadcasted_iota(jnp.int32, (tokens, 1), 0)
    for t in range(n):
        f = lax.rem(f_me + t + 1, n)
        dd, h = f // per, lax.rem(f, per)
        ii = source * per + h
        offset = h * tokens
        target = jnp.where(u_col + offset < count_s[dd], start_s[dd] + offset, -2 * loader_rows)
        pick = jnp.where(diff == target, 1.0, 0.0).astype(BF16)
        stage[t] = dot_nn(pick, rows_in[...]).astype(BF16)
        item = (stage.at[t], slots.at[f_me], s2_send.at[t], s2_recv.at[f_me], dd, ii)
        second.append((item, None))
        start_copy(*item)
        for d in range(1, reach + 1):
            item = (
                stage.at[t, :, pl.ds(qw, HD)],
                halo.at[d - 1, f_me],
                halo_send.at[d - 1, t],
                halo_recv.at[d - 1, f_me],
                dd,
                ii + d,
            )
            second.append((item, ii + d < seq_n))

            @pl.when(ii + d < seq_n)
            def _():
                start_copy(*item)

    for f in range(n):
        wait_here(slots.at[f], s2_recv.at[f])
        for d in range(1, reach + 1):

            @pl.when(i0 >= d)
            def _():
                wait_here(halo.at[d - 1, f], halo_recv.at[d - 1, f])

    bias_all = jnp.concatenate([bias] * heads, axis=0) if heads > 1 else bias

    def stacked(x):
        return jnp.concatenate([x[:, a * HD : (a + 1) * HD] for a in range(heads)], axis=0) if heads > 1 else x

    def window_of(block):
        at = block * repeat
        parts = [halo[d - 1, at] for d in range(reach, 0, -1)]
        return jnp.concatenate(parts + [slots[at][:, qw:]], axis=0)

    per_group = n // KVH
    third = []
    for g in range(KVH):
        keys = window_of(g)
        values = window_of(KVH + g)
        k_terms = None
        for f in range(g * per_group, (g + 1) * per_group):
            query = stacked(slots[f][:, :qw])
            cot = stacked(jnp.where(is_filled, g_ref[:, f * qw : (f + 1) * qw], jnp.zeros((), BF16)))
            scores = dot_nt(query, keys) * scale + bias_all
            peak = jnp.max(scores, axis=-1, keepdims=True)
            e = jnp.exp(scores - peak)
            probs = e * (1.0 / jnp.sum(e, axis=-1, keepdims=True))
            half = probs.astype(BF16)
            att = dot_nn(half, values)
            gp = dot_nt(cot, values)
            row_dot = jnp.sum(cot.astype(F32) * att, axis=-1, keepdims=True)
            gs = (probs * (gp - row_dot)).astype(BF16)
            gq = dot_nn(gs, keys) * scale
            for a in range(heads):
                cols = slice(f * qw + a * HD, f * qw + (a + 1) * HD)
                att_ref[:, cols] = att[a * tokens : (a + 1) * tokens].astype(BF16)
                gq_ref[:, cols] = gq[a * tokens : (a + 1) * tokens].astype(BF16)
            kt, vt = dot_tn(gs, query), dot_tn(half, cot)
            k_terms, v_terms = (kt, vt) if k_terms is None else (k_terms + kt, v_terms + vt)
        terms = jnp.concatenate([k_terms * scale, v_terms], axis=1)
        own_terms[g] = terms[reach * tokens :]
        for d in range(1, reach + 1):
            back_out[d - 1, g] = terms[(reach - d) * tokens : (reach - d + 1) * tokens]
            item = (
                back_out.at[d - 1, g],
                back_in.at[d - 1, g],
                back_send.at[d - 1, g],
                back_recv.at[d - 1, g],
                d0,
                i0 - d,
            )
            third.append((item, d))

            @pl.when(i0 >= d)
            def _():
                remote(*item).start()

    for g in range(KVH):
        for d in range(1, reach + 1):

            @pl.when(i0 + d < seq_n)
            def _():
                wait_here(back_in.at[d - 1, g], back_recv.at[d - 1, g])
                own_terms[g] = own_terms[g] + back_in[d - 1, g]

        both = own_terms[g].astype(BF16)
        gk_ref[:, g * HD : (g + 1) * HD] = both[:, :HD]
        gv_ref[:, g * HD : (g + 1) * HD] = both[:, HD:]

    for item in first:
        wait_sent(*item)
    for item, ok in second:
        if ok is None:
            wait_sent(*item)
        else:

            @pl.when(ok)
            def _():
                wait_sent(*item)

    for item, d in third:

        @pl.when(i0 >= d)
        def _():
            remote(*item).wait_send()


def local(queries, keys, values, doc_lengths, loader_order, grad_out):
    dp_n = lax.axis_size("dp")
    seq_n = lax.axis_size("seq")
    tokens = queries.shape[0]
    loader_rows = tokens * seq_n
    per = seq_n // dp_n
    n = dp_n * per
    reach = loader_rows // BLOCKS // tokens
    qw = QH * HD // n
    vmem = pl.BlockSpec(memory_space=pltpu.VMEM)
    smem = pl.BlockSpec(memory_space=pltpu.SMEM)
    dma = pltpu.SemaphoreType.DMA
    return pl.pallas_call(
        functools.partial(kernel, dp_n, seq_n),
        out_shape=(
            jax.ShapeDtypeStruct(queries.shape, BF16),
            jax.ShapeDtypeStruct(queries.shape, BF16),
            jax.ShapeDtypeStruct(keys.shape, BF16),
            jax.ShapeDtypeStruct(keys.shape, BF16),
        ),
        in_specs=[vmem, vmem, vmem, smem, smem, vmem],
        out_specs=(vmem, vmem, vmem, vmem),
        scratch_shapes=[
            pltpu.VMEM((tokens, 2 * KVH * HD), BF16),
            pltpu.VMEM((loader_rows, qw + HD), BF16),
            pltpu.VMEM((n, tokens, qw + HD), BF16),
            pltpu.VMEM((n, tokens, qw + HD), BF16),
            pltpu.VMEM((reach, n, tokens, HD), BF16),
            pltpu.VMEM((KVH, tokens, 2 * HD), F32),
            pltpu.VMEM((reach, KVH, tokens, 2 * HD), F32),
            pltpu.VMEM((reach, KVH, tokens, 2 * HD), F32),
            pltpu.SMEM((dp_n,), jnp.int32),
            pltpu.SMEM((dp_n,), jnp.int32),
            dma((2, n)),
            dma((2, seq_n)),
            dma((n,)),
            dma((n,)),
            dma((reach, n)),
            dma((reach, n)),
            dma((reach, KVH)),
            dma((reach, KVH)),
        ],
        compiler_params=pltpu.CompilerParams(
            collective_id=0, has_side_effects=True, vmem_limit_bytes=56 * 2**20
        ),
        name="packed_attention",
    )(queries, keys, values, doc_lengths, loader_order, grad_out)


def solution(mesh):
    rows = P(("dp", "seq"), None)
    return jax.shard_map(
        local,
        mesh=mesh,
        in_specs=(rows, rows, rows, P(), P(), rows),
        out_specs=(rows, rows, rows, rows),
        check_vma=False,
    )
```

time: 285 us -> 124 us (0.44)
  the two profiles are of different devices: /device:TPU:0 before, /device:TPU:17 now
where the time goes in v1:
time: 124 us
  Pallas kernels  118 us (95%)
  local copies, waits for them, and re-layouts  5.01 us (4%)
    pallas_call x1, Pallas kernels, local(): pl.pallas_call(functools.partial(kernel, dp_n, seq_n), out_shape=(jax.Sha...  118 us
    unnamed x10, local copies, waits for them, and re-layouts  5.01 us

profile of v1, /device:TPU:17, one launch (start us, length us, event | category | flops | bytes accessed | tf_op | source)
XLA Modules:
  0.0 123.9 jit_solution(1072543338966992227)
XLA Ops:
  0.6 118.2 %packed_attention.1 = (bf16[128,4096]{1,0:T(8,128)(2,1)}, bf16[128,4096]{1,0:T(8,128)(2,1)}, bf16[128,512]{1,0:T(8,128)(2,1)}, bf16[128,512]{1,0:T(8,128)(2,1)}) custom-call(bf16[128,4096]{1,0:T(8,128)(2,1)} %q_ref.1, bf16[128,512]{1,0:T(8,128)(2,1)} %k_ref.1, bf16[128,512]{1,0:T(8,128)(2,1)} %v_ref.1, s32[4,32]{1,0:T(4,128)} %len_ref.1, s32[4,4]{1,0:T(4,128)} %order_ref.1, ...), custom_call_target="tpu_custom_call" | custom-call | tf_op jit(solution)/shard_map/packed_attention/pallas_call | solution.py:318
  118.9 0.0 copy-start
  118.9 2.4 %copy.14 = bf16[128,4096]{1,0:T(8,128)(2,1)} copy(bf16[128,4096]{1,0:T(8,128)(2,1)} %get-tuple-element.8) | data formatting | bytes 2097152
  121.3 0.0 copy-done
  121.3 0.0 copy-start.2
  121.3 1.0 copy.15
  122.2 0.1 copy-done.2
  122.3 0.0 copy-start.1
  122.3 0.7 copy.16
  123.0 0.3 copy-done.1
  123.2 0.7 copy.17
Async XLA Ops:
  118.9 2.4 %copy-start = (bf16[128,4096]{1,0:T(8,128)(2,1)S(1)}, bf16[128,4096]{1,0:T(8,128)(2,1)}, u32[]{:S(2)}) copy-start(bf16[128,4096]{1,0:T(8,128)(2,1)} %get-tuple-element.9) | copy-start | bytes 3145732
  121.3 1.0 copy-start.2
  122.3 1.0 copy-start.1

commit v2 on v1

v2 whole, which is shorter than its diff:
```python
import functools

import jax
import jax.numpy as jnp
from jax import lax
from jax.experimental import pallas as pl
from jax.experimental.pallas import tpu as pltpu
from jax.sharding import PartitionSpec as P

QH = 32
KVH = 4
HD = 128
BLOCKS = 8
MESH = pl.DeviceIdType.MESH
F32 = jnp.float32
BF16 = jnp.bfloat16


def dot_nt(a, b):
    return lax.dot_general(a, b, (((1,), (1,)), ((), ())), preferred_element_type=F32)


def dot_nn(a, b):
    return lax.dot_general(a, b, (((1,), (0,)), ((), ())), preferred_element_type=F32)


def dot_tn(a, b):
    return lax.dot_general(a, b, (((0,), (0,)), ((), ())), preferred_element_type=F32)


def kernel(
    dp_n,
    seq_n,
    chunks,
    q_ref,
    k_ref,
    v_ref,
    len_ref,
    order_ref,
    g_ref,
    att_ref,
    gq_ref,
    gk_ref,
    gv_ref,
    parts,
    middle,
    rows_in,
    pick,
    stage,
    slots,
    halo,
    terms_sum,
    back_in,
    start_s,
    count_s,
    h1_send,
    h1_recv,
    h2_send,
    h2_recv,
    h3_send,
    h3_recv,
    halo_send,
    halo_recv,
    back_send,
    back_recv,
):
    tokens = q_ref.shape[0]
    loader_rows = tokens * seq_n
    capacity = loader_rows // dp_n
    per = capacity // tokens
    n = dp_n * per
    reach = loader_rows // BLOCKS // tokens
    qw = QH * HD // n
    heads = qw // HD
    repeat = n // (2 * KVH)
    docs = len_ref.shape[1]
    scale = HD ** (-0.5)
    d0 = lax.axis_index("dp")
    i0 = lax.axis_index("seq")
    source = i0 // per
    plane = source * per
    f_me = d0 * per + lax.rem(i0, per)

    def greet(t, carry):
        dd, ii = t // seq_n, lax.rem(t, seq_n)
        its_plane = ii // per * per
        sends = jnp.logical_and(its_plane <= i0, i0 < its_plane + per + reach)
        other = jnp.logical_or(dd != d0, ii != i0)

        @pl.when(jnp.logical_and(other, jnp.logical_or(dd == d0, sends)))
        def _():
            pl.semaphore_signal(
                pltpu.get_barrier_semaphore(), 1, device_id={"dp": dd, "seq": ii}, device_id_type=MESH
            )

        return carry

    lax.fori_loop(0, dp_n * seq_n, greet, 0)
    for f in range(n):
        c = f // repeat
        src = k_ref if c < KVH else v_ref
        c = c % KVH
        parts[f // per, f % per, 0] = src[:, c * HD : (c + 1) * HD]
        for a in range(heads):
            parts[f // per, f % per, 1 + a] = q_ref[:, f * qw + a * HD : f * qw + (a + 1) * HD]
    last = jnp.minimum(plane + per + reach, seq_n)
    pl.semaphore_wait(pltpu.get_barrier_semaphore(), seq_n - 1 + (dp_n - 1) * (last - plane))

    def remote(src, dst, send, recv, dd, ii):
        return pltpu.make_async_remote_copy(
            src_ref=src,
            dst_ref=dst,
            send_sem=send,
            recv_sem=recv,
            device_id={"dp": dd, "seq": ii},
            device_id_type=MESH,
        )

    def start_copy(src, dst, send, recv, dd, ii):
        here = jnp.logical_and(dd == d0, ii == i0)

        @pl.when(here)
        def _():
            pltpu.make_async_copy(src, dst, recv).start()

        @pl.when(jnp.logical_not(here))
        def _():
            remote(src, dst, send, recv, dd, ii).start()

    def wait_sent(src, dst, send, recv, dd, ii):
        @pl.when(jnp.logical_or(dd != d0, ii != i0))
        def _():
            remote(src, dst, send, recv, dd, ii).wait_send()

    def wait_here(dst, recv):
        pltpu.make_async_copy(dst, dst, recv).wait()

    sent = []

    def hop1(c):
        u0, m = chunks[c]
        for t in range(1, dp_n + 1):
            dd = lax.rem(d0 + t, dp_n)
            item = (
                parts.at[dd, :, pl.ds(u0, m)],
                middle.at[d0, :, pl.ds(u0, m)],
                h1_send.at[c, t - 1],
                h1_recv.at[c, d0],
                dd,
                i0,
            )
            sent.append(item)
            start_copy(*item)

    def hop2(c):
        u0, m = chunks[c]
        for d in range(dp_n):
            wait_here(middle.at[d, :, pl.ds(u0, m)], h1_recv.at[c, d])
        for t in range(1, seq_n + 1):
            ii = lax.rem(i0 + t, seq_n)
            item = (
                middle.at[ii // per, lax.rem(ii, per), pl.ds(u0, m)],
                rows_in.at[pl.ds(u0, m), i0],
                h2_send.at[c, t - 1],
                h2_recv.at[c, i0],
                d0,
                ii,
            )
            sent.append(item)
            start_copy(*item)

    def hop3(c):
        u0, m = chunks[c]
        for j in range(seq_n):
            wait_here(rows_in.at[pl.ds(u0, m), j], h2_recv.at[c, j])
        rows = [rows_in[u0 + a].reshape(loader_rows, HD) for a in range(m)]
        rows = jnp.concatenate(rows, axis=1) if m > 1 else rows[0]
        block = min(n, 8)
        for f in range(0, n, block):
            placed = dot_nn(pick[f * tokens : (f + block) * tokens], rows).astype(BF16)
            for a in range(m):
                stage[u0 + a, f : f + block] = placed[:, a * HD : (a + 1) * HD].reshape(block, tokens, HD)
        for t in range(1, n + 1):
            f = lax.rem(f_me + t, n)
            dd, ii = f // per, plane + lax.rem(f, per)
            item = (
                stage.at[pl.ds(u0, m), f],
                slots.at[pl.ds(u0, m), f_me],
                h3_send.at[c, t - 1],
                h3_recv.at[c, f_me],
                dd,
                ii,
            )
            sent.append(item)
            start_copy(*item)
        if u0 == 0:
            for item, ok in halo_items():

                @pl.when(ok)
                def _():
                    start_copy(*item)

    def halo_items():
        items = []
        for t in range(1, n + 1):
            f = lax.rem(f_me + t, n)
            dd, ii = f // per, plane + lax.rem(f, per)
            for d in range(1, reach + 1):
                item = (
                    stage.at[0, f],
                    halo.at[d - 1, f_me],
                    halo_send.at[d - 1, t - 1],
                    halo_recv.at[d - 1, f_me],
                    dd,
                    ii + d,
                )
                items.append((item, ii + d < seq_n))
        return items

    hop1(0)
    if len(chunks) > 1:
        hop1(1)

    filled = []
    for b in range(dp_n):
        total = len_ref[b, 0]
        for d in range(1, docs):
            total = total + len_ref[b, d]
        filled.append(total)
    counts = [jnp.clip(x - source * capacity, 0, capacity) for x in filled]
    order = [order_ref[source, k] for k in range(dp_n)]
    place = []
    for b in range(dp_n):
        at = jnp.int32(0)
        for k in range(dp_n):
            at = at + jnp.where(order[k] == b, k, 0)
        place.append(at)
    for b in range(dp_n):
        at = jnp.int32(0)
        for c in range(dp_n):
            at = at + jnp.where(place[c] < place[b], counts[c], 0)
        start_s[b] = at
        count_s[b] = counts[b]

    u = lax.broadcasted_iota(jnp.int32, (tokens, loader_rows), 0)
    diff = lax.broadcasted_iota(jnp.int32, (tokens, loader_rows), 1) - u
    u_col = lax.broadcasted_iota(jnp.int32, (tokens, 1), 0)
    for f in range(n):
        offset = f % per * tokens
        b = f // per
        target = jnp.where(u_col + offset < count_s[b], start_s[b] + offset, -2 * loader_rows)
        pick[f * tokens : (f + 1) * tokens] = jnp.where(diff == target, 1.0, 0.0).astype(BF16)

    row = lax.broadcasted_iota(jnp.int32, (tokens, 1), 0) + i0 * tokens
    low = jnp.zeros((tokens, 1), jnp.int32)
    end = jnp.int32(0)
    for d in range(docs):
        end = end + len_ref[d0, d]
        low = jnp.where(row >= end, end, low)
    is_filled = row < end
    low = jnp.where(is_filled, low, row)
    window = (reach + 1) * tokens
    col = lax.broadcasted_iota(jnp.int32, (tokens, window), 1) + (i0 - reach) * tokens
    allowed = jnp.logical_and(col >= low, col <= row)
    bias = jnp.where(allowed, 0.0, -jnp.inf).astype(F32)

    for d in range(1, reach + 1):

        @pl.when(i0 < d)
        def _():
            halo[d - 1] = jnp.zeros(halo.shape[1:], BF16)

    terms_sum[...] = jnp.zeros(terms_sum.shape, F32)
    per_group = n // KVH

    def window_of(block):
        at = block * repeat
        return jnp.concatenate([halo[d - 1, at] for d in range(reach, 0, -1)] + [slots[0, at]], axis=0)

    def attend(c):
        u0, m = chunks[c]
        for f in range(n):
            wait_here(slots.at[pl.ds(u0, m), f], h3_recv.at[c, f])
        if u0 == 0:
            for f in range(n):
                for d in range(1, reach + 1):

                    @pl.when(i0 >= d)
                    def _():
                        wait_here(halo.at[d - 1, f], halo_recv.at[d - 1, f])

        units = [a for a in range(u0, u0 + m) if a > 0]
        for g in range(KVH if units else 0):
            keys = window_of(g)
            values = window_of(KVH + g)
            pairs = [(f, a) for f in range(g * per_group, (g + 1) * per_group) for a in units]
            for at in range(0, len(pairs), 4):
                attend_heads(g, keys, values, pairs[at : at + 4])
            if u0 + m == heads + 1:
                send_back(g)

    def attend_heads(g, keys, values, pairs):
        h = len(pairs)
        cols = [slice(f * qw + (a - 1) * HD, f * qw + a * HD) for f, a in pairs]
        query = jnp.concatenate([slots[a, f] for f, a in pairs], axis=0)
        no = jnp.zeros((), BF16)
        cot = jnp.concatenate([jnp.where(is_filled, g_ref[:, x], no) for x in cols], axis=0)
        scores = dot_nt(query, keys) * scale + jnp.concatenate([bias] * h, axis=0)
        peak = jnp.max(scores, axis=-1, keepdims=True)
        e = jnp.exp(scores - peak)
        probs = e * (1.0 / jnp.sum(e, axis=-1, keepdims=True))
        half = probs.astype(BF16)
        att = dot_nn(half, values)
        gp = dot_nt(cot, values)
        row_dot = jnp.sum(cot.astype(F32) * att, axis=-1, keepdims=True)
        gs = (probs * (gp - row_dot)).astype(BF16)
        gq = dot_nn(gs, keys) * scale
        for at, x in enumerate(cols):
            att_ref[:, x] = att[at * tokens : (at + 1) * tokens].astype(BF16)
            gq_ref[:, x] = gq[at * tokens : (at + 1) * tokens].astype(BF16)
        terms_sum[g, :, :HD] += dot_tn(gs, query) * scale
        terms_sum[g, :, HD:] += dot_tn(half, cot)

    def back_item(d, g):
        return (
            terms_sum.at[g, pl.ds((reach - d) * tokens, tokens)],
            back_in.at[d - 1, g],
            back_send.at[d - 1, g],
            back_recv.at[d - 1, g],
            d0,
            i0 - d,
        )

    def send_back(g):
        for d in range(1, reach + 1):

            @pl.when(i0 >= d)
            def _():
                remote(*back_item(d, g)).start()

    steps = len(chunks)
    for step in range(steps + 2):
        if step < steps:
            hop2(step)
            if step + 2 < steps:
                hop1(step + 2)
        if 0 <= step - 1 < steps:
            hop3(step - 1)
        if 0 <= step - 2 < steps:
            attend(step - 2)

    for item in sent:
        wait_sent(*item)
    for item, ok in halo_items():

        @pl.when(ok)
        def _():
            wait_sent(*item)

    for g in range(KVH):
        for d in range(1, reach + 1):

            @pl.when(i0 + d < seq_n)
            def _():
                wait_here(back_in.at[d - 1, g], back_recv.at[d - 1, g])
                terms_sum[g, reach * tokens :] += back_in[d - 1, g]

        both = terms_sum[g, reach * tokens :].astype(BF16)
        gk_ref[:, g * HD : (g + 1) * HD] = both[:, :HD]
        gv_ref[:, g * HD : (g + 1) * HD] = both[:, HD:]

    for g in range(KVH):
        for d in range(1, reach + 1):

            @pl.when(i0 >= d)
            def _():
                remote(*back_item(d, g)).wait_send()


def local(queries, keys, values, doc_lengths, loader_order, grad_out):
    dp_n = lax.axis_size("dp")
    seq_n = lax.axis_size("seq")
    tokens = queries.shape[0]
    loader_rows = tokens * seq_n
    per = seq_n // dp_n
    n = dp_n * per
    reach = loader_rows // BLOCKS // tokens
    units = 1 + QH // n
    chunks = [(0, 1)] + [(u, min(2, units - u)) for u in range(1, units, 2)]
    steps = len(chunks)
    vmem = pl.BlockSpec(memory_space=pltpu.VMEM)
    smem = pl.BlockSpec(memory_space=pltpu.SMEM)
    dma = pltpu.SemaphoreType.DMA
    return pl.pallas_call(
        functools.partial(kernel, dp_n, seq_n, chunks),
        out_shape=(
            jax.ShapeDtypeStruct(queries.shape, BF16),
            jax.ShapeDtypeStruct(queries.shape, BF16),
            jax.ShapeDtypeStruct(keys.shape, BF16),
            jax.ShapeDtypeStruct(keys.shape, BF16),
        ),
        in_specs=[vmem, vmem, vmem, smem, smem, vmem],
        out_specs=(vmem, vmem, vmem, vmem),
        scratch_shapes=[
            pltpu.VMEM((dp_n, per, units, tokens, HD), BF16),
            pltpu.VMEM((dp_n, per, units, tokens, HD), BF16),
            pltpu.VMEM((units, seq_n, tokens, HD), BF16),
            pltpu.VMEM((n * tokens, loader_rows), BF16),
            pltpu.VMEM((units, n, tokens, HD), BF16),
            pltpu.VMEM((units, n, tokens, HD), BF16),
            pltpu.VMEM((reach, n, tokens, HD), BF16),
            pltpu.VMEM((KVH, (reach + 1) * tokens, 2 * HD), F32),
            pltpu.VMEM((reach, KVH, tokens, 2 * HD), F32),
            pltpu.SMEM((dp_n,), jnp.int32),
            pltpu.SMEM((dp_n,), jnp.int32),
            dma((steps, dp_n)),
            dma((steps, dp_n)),
            dma((steps, seq_n)),
            dma((steps, seq_n)),
            dma((steps, n)),
            dma((steps, n)),
            dma((reach, n)),
            dma((reach, n)),
            dma((reach, KVH)),
            dma((reach, KVH)),
        ],
        compiler_params=pltpu.CompilerParams(
            collective_id=0, has_side_effects=True, vmem_limit_bytes=60 * 2**20
        ),
        name="packed_attention",
    )(queries, keys, values, doc_lengths, loader_order, grad_out)


def solution(mesh):
    rows = P(("dp", "seq"), None)
    return jax.shard_map(
        local,
        mesh=mesh,
        in_specs=(rows, rows, rows, P(), P(), rows),
        out_specs=(rows, rows, rows, rows),
        check_vma=False,
    )
```

time: 124 us -> 68.4 us (0.55)
  Pallas kernels: 118 us -> 62.5 us
    pallas_call x1, Pallas kernels: 118 us -> 62.5 us  [local(): pl.pallas_call(functools.partial(kernel, dp_n, seq_n, chunks), out_shape=...]
where the time goes in v2:
time: 68.4 us; the launch traced here: 68.1 us
  Pallas kernels  62.5 us (91%)
  local copies, waits for them, and re-layouts  5.01 us (7%)
    pallas_call x1, Pallas kernels, local(): pl.pallas_call(functools.partial(kernel, dp_n, seq_n, chunks), out_shape=...  62.5 us
    unnamed x10, local copies, waits for them, and re-layouts  5.01 us

profile of v2, /device:TPU:17, one launch (start us, length us, event | category | flops | bytes accessed | tf_op | source)
XLA Modules:
  0.0 68.1 jit_solution(14844585404406875162)
XLA Ops:
  0.6 62.5 %packed_attention.1 = (bf16[128,4096]{1,0:T(8,128)(2,1)}, bf16[128,4096]{1,0:T(8,128)(2,1)}, bf16[128,512]{1,0:T(8,128)(2,1)}, bf16[128,512]{1,0:T(8,128)(2,1)}) custom-call(bf16[128,4096]{1,0:T(8,128)(2,1)} %q_ref.1, bf16[128,512]{1,0:T(8,128)(2,1)} %k_ref.1, bf16[128,512]{1,0:T(8,128)(2,1)} %v_ref.1, s32[4,32]{1,0:T(4,128)} %len_ref.1, s32[4,4]{1,0:T(4,128)} %order_ref.1, ...), custom_call_target="tpu_custom_call" | custom-call | tf_op jit(solution)/shard_map/packed_attention/pallas_call | solution.py:394
  63.1 0.0 copy-start
  63.1 2.4 %copy.14 = bf16[128,4096]{1,0:T(8,128)(2,1)} copy(bf16[128,4096]{1,0:T(8,128)(2,1)} %get-tuple-element.8) | data formatting | bytes 2097152
  65.5 0.0 copy-done
  65.5 0.0 copy-start.2
  65.5 1.0 %copy.15 = bf16[128,4096]{1,0:T(8,128)(2,1)} copy(bf16[128,4096]{1,0:T(8,128)(2,1)S(1)} %copy-done) | data formatting | bytes 2097152
  66.5 0.1 copy-done.2
  66.5 0.0 copy-start.1
  66.5 0.7 copy.16
  67.2 0.3 copy-done.1
  67.5 0.7 copy.17
Async XLA Ops:
  63.1 2.4 %copy-start = (bf16[128,4096]{1,0:T(8,128)(2,1)S(1)}, bf16[128,4096]{1,0:T(8,128)(2,1)}, u32[]{:S(2)}) copy-start(bf16[128,4096]{1,0:T(8,128)(2,1)} %get-tuple-element.9) | copy-start | bytes 3145732
  65.5 1.0 %copy-start.2 = (bf16[128,512]{1,0:T(8,128)(2,1)S(1)}, bf16[128,512]{1,0:T(8,128)(2,1)}, u32[]{:S(2)}) copy-start(bf16[128,512]{1,0:T(8,128)(2,1)} %get-tuple-element.10) | copy-start | bytes 393220
  66.5 1.0 %copy-start.1 = (bf16[128,512]{1,0:T(8,128)(2,1)S(1)}, bf16[128,512]{1,0:T(8,128)(2,1)}, u32[]{:S(2)}) copy-start(bf16[128,512]{1,0:T(8,128)(2,1)} %get-tuple-element.11) | copy-start | bytes 393220

commit v3 on v2

--- a/solution.py
+++ b/solution.py
@@ -50,6 +50,7 @@
     slots,
     halo,
     terms_sum,
+    back_out,
     back_in,
     start_s,
     count_s,
@@ -157,7 +158,7 @@
         for d in range(dp_n):
             wait_here(middle.at[d, :, pl.ds(u0, m)], h1_recv.at[c, d])
         for t in range(1, seq_n + 1):
-            ii = lax.rem(i0 + t, seq_n)
+            ii = lax.rem(i0 + seq_n // 2 + t, seq_n)
             item = (
                 middle.at[ii // per, lax.rem(ii, per), pl.ds(u0, m)],
                 rows_in.at[pl.ds(u0, m), i0],
@@ -323,7 +324,7 @@
 
     def back_item(d, g):
         return (
-            terms_sum.at[g, pl.ds((reach - d) * tokens, tokens)],
+            back_out.at[d - 1, g],
             back_in.at[d - 1, g],
             back_send.at[d - 1, g],
             back_recv.at[d - 1, g],
@@ -336,6 +337,7 @@
 
             @pl.when(i0 >= d)
             def _():
+                back_out[d - 1, g] = terms_sum[g, (reach - d) * tokens : (reach - d + 1) * tokens].astype(BF16)
                 remote(*back_item(d, g)).start()
 
     steps = len(chunks)
@@ -363,7 +365,7 @@
             @pl.when(i0 + d < seq_n)
             def _():
                 wait_here(back_in.at[d - 1, g], back_recv.at[d - 1, g])
-                terms_sum[g, reach * tokens :] += back_in[d - 1, g]
+                terms_sum[g, reach * tokens :] += back_in[d - 1, g].astype(F32)
 
         both = terms_sum[g, reach * tokens :].astype(BF16)
         gk_ref[:, g * HD : (g + 1) * HD] = both[:, :HD]
@@ -410,7 +412,8 @@
             pltpu.VMEM((units, n, tokens, HD), BF16),
             pltpu.VMEM((reach, n, tokens, HD), BF16),
             pltpu.VMEM((KVH, (reach + 1) * tokens, 2 * HD), F32),
-            pltpu.VMEM((reach, KVH, tokens, 2 * HD), F32),
+            pltpu.VMEM((reach, KVH, tokens, 2 * HD), BF16),
+            pltpu.VMEM((reach, KVH, tokens, 2 * HD), BF16),
             pltpu.SMEM((dp_n,), jnp.int32),
             pltpu.SMEM((dp_n,), jnp.int32),
             dma((steps, dp_n)),

time: 68.4 us -> 66.5 us (0.972)
  Pallas kernels: 62.5 us -> 60.4 us
    pallas_call x1, Pallas kernels: 62.5 us -> 60.4 us  [local(): pl.pallas_call(functools.partial(kernel, dp_n, seq_n, chunks), out_shape=...]
where the time goes in v3:
time: 66.5 us; the launch traced here: 66 us
  Pallas kernels  60.4 us (91%)
  local copies, waits for them, and re-layouts  5.01 us (8%)
    pallas_call x1, Pallas kernels, local(): pl.pallas_call(functools.partial(kernel, dp_n, seq_n, chunks), out_shape=...  60.4 us
    unnamed x10, local copies, waits for them, and re-layouts  5.01 us

profile of v3, /device:TPU:17, one launch (start us, length us, event | category | flops | bytes accessed | tf_op | source)
XLA Modules:
  0.0 66.0 jit_solution(3134726018483576321)
XLA Ops:
  0.6 60.4 %packed_attention.1 = (bf16[128,4096]{1,0:T(8,128)(2,1)}, bf16[128,4096]{1,0:T(8,128)(2,1)}, bf16[128,512]{1,0:T(8,128)(2,1)}, bf16[128,512]{1,0:T(8,128)(2,1)}) custom-call(bf16[128,4096]{1,0:T(8,128)(2,1)} %q_ref.1, bf16[128,512]{1,0:T(8,128)(2,1)} %k_ref.1, bf16[128,512]{1,0:T(8,128)(2,1)} %v_ref.1, s32[4,32]{1,0:T(4,128)} %len_ref.1, s32[4,4]{1,0:T(4,128)} %order_ref.1, ...), custom_call_target="tpu_custom_call" | custom-call | tf_op jit(solution)/shard_map/packed_attention/pallas_call | solution.py:396
  61.0 0.0 copy-start
  61.0 2.4 %copy.14 = bf16[128,4096]{1,0:T(8,128)(2,1)} copy(bf16[128,4096]{1,0:T(8,128)(2,1)} %get-tuple-element.8) | data formatting | bytes 2097152
  63.4 0.0 copy-done
  63.4 0.0 copy-start.2
  63.4 1.0 %copy.15 = bf16[128,4096]{1,0:T(8,128)(2,1)} copy(bf16[128,4096]{1,0:T(8,128)(2,1)S(1)} %copy-done) | data formatting | bytes 2097152
  64.4 0.1 copy-done.2
  64.4 0.0 copy-start.1
  64.4 0.7 copy.16
  65.1 0.3 copy-done.1
  65.4 0.7 copy.17
Async XLA Ops:
  61.0 2.4 %copy-start = (bf16[128,4096]{1,0:T(8,128)(2,1)S(1)}, bf16[128,4096]{1,0:T(8,128)(2,1)}, u32[]{:S(2)}) copy-start(bf16[128,4096]{1,0:T(8,128)(2,1)} %get-tuple-element.9) | copy-start | bytes 3145732
  63.4 1.0 %copy-start.2 = (bf16[128,512]{1,0:T(8,128)(2,1)S(1)}, bf16[128,512]{1,0:T(8,128)(2,1)}, u32[]{:S(2)}) copy-start(bf16[128,512]{1,0:T(8,128)(2,1)} %get-tuple-element.10) | copy-start | bytes 393220
  64.4 1.0 %copy-start.1 = (bf16[128,512]{1,0:T(8,128)(2,1)S(1)}, bf16[128,512]{1,0:T(8,128)(2,1)}, u32[]{:S(2)}) copy-start(bf16[128,512]{1,0:T(8,128)(2,1)} %get-tuple-element.11) | copy-start | bytes 393220

commit v4 on v3

--- a/solution.py
+++ b/solution.py
@@ -155,10 +155,11 @@
 
     def hop2(c):
         u0, m = chunks[c]
-        for d in range(dp_n):
-            wait_here(middle.at[d, :, pl.ds(u0, m)], h1_recv.at[c, d])
         for t in range(1, seq_n + 1):
-            ii = lax.rem(i0 + seq_n // 2 + t, seq_n)
+            d = lax.rem(d0 + dp_n - (t - 1) // per, dp_n)
+            if (t - 1) % per == 0:
+                wait_here(middle.at[d, :, pl.ds(u0, m)], h1_recv.at[c, d])
+            ii = d * per + lax.rem(i0 + t, per)
             item = (
                 middle.at[ii // per, lax.rem(ii, per), pl.ds(u0, m)],
                 rows_in.at[pl.ds(u0, m), i0],

time: 66.5 us -> 65.5 us (0.985)
  the two profiles are of different devices: /device:TPU:17 before, /device:TPU:9 now
where the time goes in v4:
time: 65.5 us; the launch traced here: 65.3 us
  Pallas kernels  59.6 us (91%)
  local copies, waits for them, and re-layouts  5.01 us (8%)
    pallas_call x1, Pallas kernels, local(): pl.pallas_call(functools.partial(kernel, dp_n, seq_n, chunks), out_shape=...  59.6 us
    unnamed x10, local copies, waits for them, and re-layouts  5.01 us

profile of v4, /device:TPU:9, one launch (start us, length us, event | category | flops | bytes accessed | tf_op | source)
XLA Modules:
  0.0 65.3 jit_solution(12791333047784673259)
XLA Ops:
  0.6 59.6 %packed_attention.1 = (bf16[128,4096]{1,0:T(8,128)(2,1)}, bf16[128,4096]{1,0:T(8,128)(2,1)}, bf16[128,512]{1,0:T(8,128)(2,1)}, bf16[128,512]{1,0:T(8,128)(2,1)}) custom-call(bf16[128,4096]{1,0:T(8,128)(2,1)} %q_ref.1, bf16[128,512]{1,0:T(8,128)(2,1)} %k_ref.1, bf16[128,512]{1,0:T(8,128)(2,1)} %v_ref.1, s32[4,32]{1,0:T(4,128)} %len_ref.1, s32[4,4]{1,0:T(4,128)} %order_ref.1, ...), custom_call_target="tpu_custom_call" | custom-call | tf_op jit(solution)/shard_map/packed_attention/pallas_call | solution.py:397
  60.3 0.0 copy-start
  60.3 2.4 %copy.14 = bf16[128,4096]{1,0:T(8,128)(2,1)} copy(bf16[128,4096]{1,0:T(8,128)(2,1)} %get-tuple-element.8) | data formatting | bytes 2097152
  62.7 0.0 copy-done
  62.7 0.0 copy-start.2
  62.7 1.0 %copy.15 = bf16[128,4096]{1,0:T(8,128)(2,1)} copy(bf16[128,4096]{1,0:T(8,128)(2,1)S(1)} %copy-done) | data formatting | bytes 2097152
  63.6 0.1 copy-done.2
  63.7 0.0 copy-start.1
  63.7 0.7 %copy.16 = bf16[128,512]{1,0:T(8,128)(2,1)} copy(bf16[128,512]{1,0:T(8,128)(2,1)S(1)} %copy-done.2) | data formatting | bytes 262144
  64.4 0.3 copy-done.1
  64.6 0.7 %copy.17 = bf16[128,512]{1,0:T(8,128)(2,1)} copy(bf16[128,512]{1,0:T(8,128)(2,1)S(1)} %copy-done.1) | data formatting | bytes 262144
Async XLA Ops:
  60.3 2.4 %copy-start = (bf16[128,4096]{1,0:T(8,128)(2,1)S(1)}, bf16[128,4096]{1,0:T(8,128)(2,1)}, u32[]{:S(2)}) copy-start(bf16[128,4096]{1,0:T(8,128)(2,1)} %get-tuple-element.9) | copy-start | bytes 3145732
  62.7 1.0 %copy-start.2 = (bf16[128,512]{1,0:T(8,128)(2,1)S(1)}, bf16[128,512]{1,0:T(8,128)(2,1)}, u32[]{:S(2)}) copy-start(bf16[128,512]{1,0:T(8,128)(2,1)} %get-tuple-element.10) | copy-start | bytes 393220
  63.7 1.0 %copy-start.1 = (bf16[128,512]{1,0:T(8,128)(2,1)S(1)}, bf16[128,512]{1,0:T(8,128)(2,1)}, u32[]{:S(2)}) copy-start(bf16[128,512]{1,0:T(8,128)(2,1)} %get-tuple-element.11) | copy-start | bytes 393220
